TPU v7x, 256 devices: a whole 4x4x8 slice. The times are simulated.
256 devices in a mesh: node: 256 (over z, x, y, core).
Axes of the slice: x: 4, y: 4, z: 8, core: 2. Of those that a mesh axis runs over, the one named last changes fastest.
Arguments:
- embed: float32 [1048576, 128], P('node')
- tiles: bfloat16 [49152, 128, 128], P('node'), may hold values from -0.21875 to 0.21875
- tile_rows: int32 [49152], P('node'), may hold values from 0 to 31
- tile_cols: int32 [49152], P('node'), may hold values from 0 to 8191, as said below
- tile_count: int32 [256], P('node'), may hold values from 48 to 192, as said below
Outputs:
- spectral: float32 [1048576, 128], P('node')
Inputs may be any that keep to these rules, and one draw needn't show every extreme that they name: `tile_cols`: slot s of device d names one of device d's own blocks, one of the last 16 blocks of device d - 1, or one of the first 16 blocks of device d + 1 (devices counted around the cycle); the first slot of every device names a block of device d - 1 and the second one of device d + 1. `tile_count`: some device has all 192 slots live.
All inputs are finite; a program needn't handle non-finite values.
Results may differ from a plain program's by a relative error of at most 0.003.
Values may be sent and summed in bfloat16 or wider, within the bound.
No kernel may reach another device: no remote copies, remote signals or barrier semaphores. Data moves between devices by JAX's collectives and lax.ppermute only.
A program may use at most 128 MiB of HBM per device.

v0:
```python
import jax
import jax.numpy as jnp
from jax import lax
from jax.sharding import PartitionSpec as P

spectral_shift = 0.5
weight_zero = 0.6
weight_one = -0.9
weight_two = 0.45


def extended_2(shard, sides, width):
    for axis, dim in sides:
        size, length = (lax.axis_size(axis), shard.shape[dim])
        up = [(i, (i + 1) % size) for i in range(size)]
        down = [(j, i) for i, j in up]
        last = lax.slice_in_dim(shard, length - width, length, axis=dim)
        initial = lax.slice_in_dim(shard, 0, width, axis=dim)
        before = lax.ppermute(last, axis, up)
        after = lax.ppermute(initial, axis, down)
        shard = jnp.concatenate([before, shard, after], axis=dim)
    return shard


def tile_products(tiles, source, local_cols):
    picked = jnp.take(source, local_cols, axis=0)
    return jnp.einsum("tij,tjf->tif", tiles, picked, preferred_element_type=jnp.float32)


def propagate(field, tiles, tile_rows, tile_cols, tile_count):
    block_size = tiles.shape[1]
    width = field.shape[1]
    slot_count = tiles.shape[0]
    own_blocks = field.shape[0] // block_size
    edge_blocks = own_blocks // 2
    rounded = field.astype(jnp.bfloat16)
    nblocks = own_blocks * lax.axis_size("node")
    first_block = lax.axis_index("node") * own_blocks
    local_cols = (tile_cols - first_block + edge_blocks) % nblocks
    extended = extended_2(rounded, (("node", 0),), edge_blocks * block_size)
    extended = extended.reshape(-1, block_size, width)
    product = tile_products(tiles, extended, local_cols)
    alive = (jnp.arange(slot_count) < tile_count[0]).astype(jnp.float32)
    selector = (tile_rows[None, :] == jnp.arange(own_blocks)[:, None]).astype(jnp.float32) * alive[
        None, :
    ]
    flat = product.reshape(slot_count, block_size * width)
    summed = jnp.dot(
        selector, flat, precision=lax.Precision.HIGHEST, preferred_element_type=jnp.float32
    )
    return summed.reshape(own_blocks * block_size, width) - spectral_shift * field


def inner_gram(left, right):
    return jnp.dot(
        left.T, right, precision=lax.Precision.HIGHEST, preferred_element_type=jnp.float32
    )


def local(embed, tiles, tile_rows, tile_cols, tile_count):
    first = propagate(embed, tiles, tile_rows, tile_cols, tile_count)
    partial_mix = weight_zero * embed + weight_one * first
    second = 2.0 * propagate(first, tiles, tile_rows, tile_cols, tile_count) - embed
    mixed = partial_mix + weight_two * second
    gram = lax.psum(inner_gram(mixed, mixed), "node")
    lower = jnp.linalg.cholesky(gram)
    solved = jax.scipy.linalg.solve_triangular(lower, mixed.T, lower=True).T
    total_rows = embed.shape[0] * lax.axis_size("node")
    return solved * jnp.sqrt(jnp.float32(total_rows))


def solution(mesh):
    return jax.shard_map(
        local,
        mesh=mesh,
        in_specs=(P("node", None), P("node", None, None), P("node"), P("node"), P("node")),
        out_specs=P("node", None),
        check_vma=False,
    )
```

profile of v0, /device:TPU:4, one launch (start us, length us, event | category | flops | bytes accessed | tf_op | source)
XLA Modules:
  0.0 442.8 jit_solution(13791125124305239474)
XLA Ops:
  6.5 0.0 copy-start.4
  6.5 0.0 all-reduce.2.cloned.1.call-start
  6.5 1.7 convert_element_type.17
  8.2 0.1 fusion.39
  8.3 0.1 collective-permute-start
  8.4 3.8 collective-permute-start.1
  12.9 0.0 copy-done.4
  13.0 6.2 %collective-permute-done = bf16[2048,128]{1,0:T(8,128)(2,1)S(1)} collective-permute-done((bf16[2048,128]{1,0:T(8,128)(2,1)S(1)}, bf16[2048,128]{1,0:T(8,128)(2,1)S(1)}, u32[]{:S(2)}, u32[]{:S(2)}) %collective-permute-start) | collective-permute-done | bytes 524320 | tf_op jit(solution)/shard_map/ppermute | solution.py:19
  19.1 0.0 copy-start.2
  19.1 0.8 copy-done.2
  19.9 0.0 collective-permute-done.1
  19.9 1.3 pad_maximum_fusion
  21.3 8.0 %gather_fusion = bf16[192,128,128]{2,1,0:T(8,128)(2,1)} fusion(bf16[64,128,128]{2,1,0:T(8,128)(2,1)S(1)} %bitcast.30, s32[1024]{0:T(1024)S(1)} %pad_clamp_fusion), kind=kCustom, calls=%fused_computation.clone | custom fusion | bytes 12583680 | tf_op jit(solution)/shard_map/jit(_take)/gather | solution.py:26
  29.3 13.8 %fusion.12 = f32[192,128,128]{1,2,0:T(8,128)} fusion(bf16[192,128,128]{2,1,0:T(8,128)(2,1)} %param.8, bf16[192,128,128]{2,1,0:T(8,128)(2,1)} %gather_fusion, pred[192]{0:T(512)(128)(4,1)S(1)} %get-tuple-element.6), kind=kOutput, calls=%fused_computation.15 | convolution fusion | flops 808452096 | bytes 25166016 | tf_op jit(solution)/shard_map/tij,tjf->tif/dot_general | solution.py:27
  43.0 0.0 copy-start.3
  43.0 12.6 %copy.9 = f32[192,128,128]{2,1,0:T(8,128)} copy(f32[192,128,128]{1,2,0:T(8,128)} %fusion.12) | data formatting | bytes 25165824 | tf_op jit(solution)/shard_map/tij,tjf->tif/dot_general | solution.py:27
  55.6 0.0 copy-done.3
  55.6 20.7 %fusion.3 = f32[32,16384]{1,0:T(8,128)} fusion(f32[24,8,128,128]{3,2,1,0:T(8,128)} %bitcast.28, f32[192]{0:T(256)S(1)} %compare_convert_fusion, s32[192]{0:T(256)S(1)} %copy-done.3), kind=kOutput, calls=%fused_computation.5 | convolution fusion | flops 1207971840 | bytes 14681600 | tf_op jit(solution)/shard_map/dot_general | solution.py:48
  76.3 0.0 copy-start
  76.3 2.9 reshape.41
  79.2 0.0 copy-done
  79.2 1.8 fusion.20
  81.0 0.1 fusion.38
  81.1 0.1 collective-permute-start.2
  81.2 3.8 collective-permute-start.3
  85.1 6.9 %collective-permute-done.2 = bf16[2048,128]{1,0:T(8,128)(2,1)S(1)} collective-permute-done((bf16[2048,128]{1,0:T(8,128)(2,1)S(1)}, bf16[2048,128]{1,0:T(8,128)(2,1)S(1)}, u32[]{:S(2)}, u32[]{:S(2)}) %collective-permute-start.2) | collective-permute-done | bytes 524320 | tf_op jit(solution)/shard_map/ppermute | solution.py:19
  91.9 0.0 collective-permute-done.3
  91.9 0.1 pad_maximum_fusion.1
  92.1 8.2 %gather_fusion.1 = bf16[192,128,128]{2,1,0:T(8,128)(2,1)} fusion(bf16[64,128,128]{2,1,0:T(8,128)(2,1)S(1)} %bitcast.29, s32[1024]{0:T(1024)S(1)} %pad_clamp_fusion), kind=kCustom, calls=%fused_computation.1.clone | custom fusion | bytes 12583680 | tf_op jit(solution)/shard_map/jit(_take)/gather | solution.py:26
  100.2 13.8 %fusion.15 = f32[192,128,128]{1,2,0:T(8,128)} fusion(bf16[192,128,128]{2,1,0:T(8,128)(2,1)} %param.8, bf16[192,128,128]{2,1,0:T(8,128)(2,1)} %gather_fusion.1, pred[192]{0:T(512)(128)(4,1)S(1)} %get-tuple-element.6), kind=kOutput, calls=%fused_computation.16 | convolution fusion | flops 808452096 | bytes 25166016 | tf_op jit(solution)/shard_map/tij,tjf->tif/dot_general | solution.py:27
  114.0 12.6 %copy.11 = f32[192,128,128]{2,1,0:T(8,128)} copy(f32[192,128,128]{1,2,0:T(8,128)} %fusion.15) | data formatting | bytes 25165824 | tf_op jit(solution)/shard_map/tij,tjf->tif/dot_general | solution.py:27
  126.6 20.4 %fusion = f32[32,16384]{1,0:T(8,128)} fusion(f32[24,8,128,128]{3,2,1,0:T(8,128)} %bitcast.27, f32[192]{0:T(256)S(1)} %compare_convert_fusion, s32[192]{0:T(256)S(1)} %copy-done.3), kind=kOutput, calls=%fused_computation.2 | convolution fusion | flops 1207971840 | bytes 14681600 | tf_op jit(solution)/shard_map/dot_general | solution.py:48
  147.0 0.0 copy-start.1
  147.0 3.1 reshape.44
  150.2 0.0 copy-done.1
  150.2 8.9 %fusion.37 = f32[128,128]{0,1:T(8,128)} fusion(f32[4096,128]{1,0:T(8,128)S(1)} %copy-done.1, f32[4096,128]{1,0:T(8,128)} %reshape.44, f32[4096,128]{1,0:T(8,128)} %reshape.41), kind=kOutput, calls=%fused_computation.54 | convolution fusion | flops 811073536 | bytes 6356992 | tf_op jit(solution)/shard_map/dot_general | solution.py:55
  159.1 0.0 all-reduce.2.cloned.1.call-update
  159.1 245.8 %all-reduce.2.cloned.1.call-done = f32[128,128]{0,1:T(8,128)} async-done(((f32[128,128]{0,1:T(8,128)}), f32[128,128]{0,1:T(8,128)}) %all-reduce.2.cloned.1.call-update) | async-done | bytes 65552 | tf_op jit(solution)/shard_map/psum | solution.py:65
  405.0 0.9 copy.13
  405.9 0.9 fusion.23
  406.8 11.7 %cholesky.16 = f32[128,128]{1,0:T(8,128)S(1)} custom-call(f32[128,128]{1,0:T(8,128)S(1)} %fusion.23), custom_call_target="Cholesky" | custom-call | tf_op jit(solution)/shard_map/jit(cholesky)/cholesky | solution.py:66
  418.5 0.6 compare_reduce_fusion
  419.2 0.7 fusion.21
  419.8 9.8 %custom-call.7 = f32[1,128,128]{1,2,0:T(8,128)S(1)} custom-call(f32[1,128,128]{2,1,0:T(8,128)S(1)} %fusion.21), custom_call_target="InvertDiagBlocksLowerTriangular" | custom-call | tf_op jit(solution)/shard_map/jit(_solve_triangular)/triangular_solve | solution.py:67
  429.7 5.9 %convolution_multiply_fusion = f32[4096,128]{1,0:T(8,128)} fusion(f32[1,128,128]{1,2,0:T(8,128)S(1)} %custom-call.7, f32[4096,128]{1,0:T(8,128)S(1)} %copy-done.1, f32[4096,128]{1,0:T(8,128)} %reshape.44, f32[4096,128]{1,0:T(8,128)} %reshape.41), kind=kOutput, calls=%fused_computation.14 | convolution fusion | flops 811597824 | bytes 8454144 | tf_op jit(solution)/shard_map/jit(_solve_triangular)/triangular_solve | solution.py:67
  (4 shorter events, 0.1 us)
Async XLA Ops:
  6.5 6.4 %copy-start.4 = (s32[192]{0:T(256)S(1)}, s32[192]{0:T(256)}, u32[]{:S(2)}) copy-start(s32[192]{0:T(256)} %param.10) | copy-start | bytes 2308
  6.5 398.5 %all-reduce.2.cloned.1.call-start = ((), (), s32[]{:S(2)}) async-start(), calls=%async_computation | async-start | bytes 131072 | tf_op jit(solution)/shard_map/psum | solution.py:65
  8.3 10.8 %collective-permute-start = (bf16[2048,128]{1,0:T(8,128)(2,1)S(1)}, bf16[2048,128]{1,0:T(8,128)(2,1)S(1)}, u32[]{:S(2)}, u32[]{:S(2)}) collective-permute-start(bf16[2048,128]{1,0:T(8,128)(2,1)S(1)} %get-tuple-element.10), channel_id=1, source_target_pairs={{0,1},{1,2},{2,3},{3,4},{4,5},{5,6},{6,7},{7,8},{8,9},{9,10},{10,1... | collective-permute-start | bytes 1572872 | tf_op jit(solution)/shard_map/ppermute | solution.py:19
  8.4 11.5 %collective-permute-start.1 = (bf16[2048,128]{1,0:T(8,128)(2,1)S(1)}, bf16[2048,128]{1,0:T(8,128)(2,1)}, u32[]{:S(2)}, u32[]{:S(2)}) collective-permute-start(bf16[2048,128]{1,0:T(8,128)(2,1)S(1)} %get-tuple-element.11), channel_id=1, source_target_pairs={{1,0},{2,1},{3,2},{4,3},{5,4},{6,5},{7,6},{8,7},{9,8},{10,9},{11,1... | collective-permute-start | bytes 1572872 | tf_op jit(solution)/shard_map/ppermute | solution.py:20
  19.1 0.8 copy-start.2
  43.0 12.6 %copy-start.3 = (s32[192]{0:T(256)S(1)}, s32[192]{0:T(256)}, u32[]{:S(2)}) copy-start(s32[192]{0:T(256)} %param.9) | copy-start | bytes 2308
  76.3 2.9 copy-start
  81.1 10.8 %collective-permute-start.2 = (bf16[2048,128]{1,0:T(8,128)(2,1)S(1)}, bf16[2048,128]{1,0:T(8,128)(2,1)S(1)}, u32[]{:S(2)}, u32[]{:S(2)}) collective-permute-start(bf16[2048,128]{1,0:T(8,128)(2,1)S(1)} %get-tuple-element.8), channel_id=1, source_target_pairs={{0,1},{1,2},{2,3},{3,4},{4,5},{5,6},{6,7},{7,8},{8,9},{9,10},{10,1... | collective-permute-start | bytes 1572872 | tf_op jit(solution)/shard_map/ppermute | solution.py:19
  81.2 10.7 %collective-permute-start.3 = (bf16[2048,128]{1,0:T(8,128)(2,1)S(1)}, bf16[2048,128]{1,0:T(8,128)(2,1)S(1)}, u32[]{:S(2)}, u32[]{:S(2)}) collective-permute-start(bf16[2048,128]{1,0:T(8,128)(2,1)S(1)} %get-tuple-element.9), channel_id=1, source_target_pairs={{1,0},{2,1},{3,2},{4,3},{5,4},{6,5},{7,6},{8,7},{9,8},{10,9},{11,1... | collective-permute-start | bytes 1572872 | tf_op jit(solution)/shard_map/ppermute | solution.py:20
  147.0 3.1 copy-start.1
Sparse Core Ops, SparseCore 0:
  159.3 245.6 all-reduce.1
where the time goes:
time: 452 us; the launch traced here: 443 us
  waiting for transfers between devices  259 us (57%)
  matrix products  83.5 us (18%)
  local copies, waits for them, and re-layouts  49.2 us (11%)
  other arithmetic  28.7 us (6%)
  between operations  14.6 us (3%)
  starting transfers between devices  7.85 us (2%)
    psum x1, waiting for transfers between devices, local(): gram = lax.psum(inner_gram(mixed, mixed), 'node')  246 us
    dot_general x2, matrix products, propagate(): jnp.dot(selector, flat, precision=lax.Precision.HIGHEST, preferred_elemen...  41.1 us
    dot_general x2, matrix products, tile_products(): jnp.einsum('tij,tjf->tif', tiles, picked, preferred_element_type=jnp.floa...  27.5 us
    dot_general x2, local copies, waits for them, and re-layouts, tile_products(): jnp.einsum('tij,tjf->tif', tiles, picked, preferred_element_type=jnp.floa...  25.2 us
    gather x2, local copies, waits for them, and re-layouts, tile_products(): picked = jnp.take(source, local_cols, axis=0)  16.2 us
    ppermute x2, waiting for transfers between devices, extended_2(): before = lax.ppermute(last, axis, up)  13 us
    another operation x3, other arithmetic, local(): lower = jnp.linalg.cholesky(gram)  12.4 us
    another operation x2, other arithmetic, local(): solved = jax.scipy.linalg.solve_triangular(lower, mixed.T, lower=True).T  10.5 us
  transfers between devices with their start and end apart: 5, of which 3 were waited for; matrix products, arithmetic and copies ran while one was open for 0% of the time, Pallas kernels for 0%

commit v1 on v0

v1 whole, which is shorter than its diff:
```python
import jax
import jax.numpy as jnp
from jax import lax
from jax.experimental import pallas as pl
from jax.experimental.pallas import tpu as pltpu
from jax.sharding import PartitionSpec as P

BS = 128
OWN = 32
HALF = 16
SLOTS = 192
LISTLEN = 256
GROUP = 4
PANEL = 16
MIB = 1024 * 1024

F32 = jnp.float32
BF16 = jnp.bfloat16

spectral_shift = 0.5
weight_zero = 0.6
weight_one = -0.9
weight_two = 0.45
c_embed = weight_zero - weight_two
c_sum = 2.0 * weight_two
c_first = weight_one - c_sum * spectral_shift


def vmem(*shape, dtype):
    return pltpu.VMEM(shape, dtype)


def in_vmem(array):
    return pltpu.with_memory_space_constraint(array, pltpu.VMEM)


V = pl.BlockSpec(memory_space=pltpu.VMEM)
S = pl.BlockSpec(memory_space=pltpu.SMEM)
H = pl.BlockSpec(memory_space=pl.ANY)


def params(mib):
    return pltpu.CompilerParams(vmem_limit_bytes=mib * MIB)


def cost(flops, moved):
    return pl.CostEstimate(flops=flops, bytes_accessed=moved, transcendentals=0)


def slot_lists(tile_rows, tile_cols, tile_count, device, flip, size):
    i32 = jnp.int32
    core = device % 2
    local = (tile_cols - device * OWN + HALF) % (OWN * size)
    own = (local >= HALF) & (local < HALF + OWN)
    after = (local >= HALF + OWN).astype(i32)
    source = jnp.where(own, (local - HALF) ^ flip, local - 48 * after + HALF * (after ^ core))
    row = tile_rows ^ flip
    slots = jnp.arange(SLOTS, dtype=i32)
    alive = slots < tile_count[0]
    bucket = jnp.where(alive, jnp.where(own, row, row + OWN), 2 * OWN)
    code = slots | (source << 8) | (row << 16)
    same = bucket[:, None] == bucket[None, :]
    rank = jnp.sum((same & (slots[None, :] < slots[:, None])).astype(i32), axis=1)
    buckets = jnp.arange(2 * OWN, dtype=i32)
    count = jnp.sum((bucket[None, :] == buckets[:, None]).astype(i32), axis=1)
    pairs = (count + 1) // 2
    earlier = (buckets[None, :] < bucket[:, None]) & ((buckets[None, :] >= OWN) == (bucket[:, None] >= OWN))
    start = jnp.sum(jnp.where(earlier, 2 * pairs[None, :], 0), axis=1)
    place = jnp.where(alive, start + rank + jnp.where(bucket >= OWN, LISTLEN, 0), -1)
    places = jnp.arange(2 * LISTLEN, dtype=i32)
    hit = place[None, :] == places[:, None]
    order = SLOTS + jnp.sum(jnp.where(hit, code[None, :] - SLOTS, 0), axis=1)
    n_own = jnp.sum(pairs[:OWN])
    n_cross = jnp.sum(pairs[OWN : OWN + HALF])
    n_halo = jnp.sum(pairs[OWN:])
    meta = jnp.stack([flip, n_own, n_cross, n_halo]).astype(i32)
    return order, meta


def tile_sums(order, start, stop, source, tiles, total):
    def group(g, carry):
        products = []
        for u in range(GROUP):
            at = start + 2 * (g * GROUP + u)
            first, second = order[at], order[at + 1]
            wide = jnp.concatenate([tiles[first & 255], tiles[second & 255]], axis=1)
            tall = jnp.concatenate([source[(first >> 8) & 255], source[(second >> 8) & 255]], axis=0)
            products.append((first >> 16, jnp.dot(wide, tall, preferred_element_type=F32)))
        for row, product in products:
            total[row] += product
        return carry

    lax.fori_loop(0, (stop + GROUP - 1) // GROUP, group, 0)


def own_first_kernel(order, meta, cross, inner, embed, tiles, total, kept, source, sem):
    flip = meta[0]
    halves = [
        pltpu.make_async_copy(
            embed.at[pl.ds(h * HALF ^ flip, HALF)], total.at[pl.ds(h * HALF, HALF)], sem.at[h]
        )
        for h in range(2)
    ]
    tile_copy = pltpu.make_async_copy(tiles, kept.at[pl.ds(0, SLOTS)], sem.at[2])
    for copy in halves:
        copy.start()
    tile_copy.start()
    kept[SLOTS] = jnp.zeros((BS, BS), BF16)
    source[:HALF] = cross[...]
    source[HALF:] = inner[...]
    for copy in halves:
        copy.wait()
    total[...] = total[...] * (-spectral_shift)
    tile_copy.wait()
    tile_sums(order, 0, meta[1], source, kept, total)


def halo_first_kernel(order, meta, cross, inner, tiles, before, total, out_cross, out_inner, source):
    source[:HALF] = cross[...]
    source[HALF:] = inner[...]
    total[...] = before[...]
    tile_sums(order, LISTLEN, meta[3], source, tiles, total)
    out_cross[...] = total[:HALF].astype(BF16)
    out_inner[...] = total[HALF:].astype(BF16)


def own_second_kernel(order, meta, cross, inner, tiles, first, total, source):
    source[:HALF] = cross[...]
    source[HALF:] = inner[...]
    total[...] = first[...] * (c_first / c_sum)
    tile_sums(order, 0, meta[1], source, tiles, total)


def halo_second_kernel(order, meta, cross, inner, tiles, before, embed, split, gram, source, total, field, sem):
    flip = meta[0]
    halves = [
        pltpu.make_async_copy(
            embed.at[pl.ds(h * HALF ^ flip, HALF)], field.at[pl.ds(h * HALF, HALF)], sem.at[h]
        )
        for h in range(2)
    ]
    for copy in halves:
        copy.start()
    source[:HALF] = cross[...]
    source[HALF:] = inner[...]
    total[...] = before[...]
    tile_sums(order, LISTLEN, meta[3], source, tiles, total)
    for copy in halves:
        copy.wait()

    def block(g, sums):
        mixed = c_sum * total[pl.ds(2 * g, 2)] + c_embed * field[pl.ds(2 * g, 2)]
        mixed = mixed.reshape(2 * BS, BS)
        high = mixed.astype(BF16)
        low = (mixed - high.astype(F32)).astype(BF16)
        both = jnp.concatenate([high, low], axis=1)
        split[g] = both
        return sums + lax.dot_general(high, both, (((0,), (0,)), ((), ())), preferred_element_type=F32)

    sums = lax.fori_loop(0, OWN // 2, block, jnp.zeros((BS, 2 * BS), F32))
    gram[...] = sums[:, :BS] + (sums[:, BS:] + sums[:, BS:].T)


def three_parts(x):
    high = x.astype(BF16)
    rest = x - high.astype(F32)
    middle = rest.astype(BF16)
    low = (rest - middle.astype(F32)).astype(BF16)
    return high, middle, low


def inverse_factor(gram, work):
    n = BS
    rows = lax.broadcasted_iota(jnp.int32, (n, n), 0)
    columns = lax.broadcasted_iota(jnp.int32, (n, n), 1)
    work[:, :n] = gram
    work[:, n:] = jnp.where(rows == columns, 1.0, 0.0).astype(F32)
    place = lax.broadcasted_iota(jnp.int32, (PANEL, n), 0)
    for base in range(0, n, PANEL):
        panel = work[base : base + PANEL, :]
        left, right = panel[:, :n], panel[:, n:]
        spread = [
            jnp.broadcast_to(left[:, base + k : base + k + 1], (PANEL, n)) for k in range(PANEL)
        ]
        scale = jnp.zeros((PANEL, n), F32)
        for j in range(PANEL):
            inverse = 1.0 / spread[j][j : j + 1, :]
            scale = jnp.where(place == j, inverse, scale)
            if j + 1 < PANEL:
                factor = jnp.where(place > j, spread[j] * inverse, 0.0)
                for k in range(j + 1, PANEL):
                    spread[k] = spread[k] - factor * spread[k][j : j + 1, :]
                left = left - factor * left[j : j + 1, :]
                right = right - factor * right[j : j + 1, :]
        if base + PANEL < n:
            ah, am, al = three_parts(left * scale)
            both = jnp.concatenate([left, right], axis=1)
            bh, bm, bl = three_parts(both)
            update = lax.dot_general(
                jnp.concatenate([ah, ah, am, am, ah, al], axis=0),
                jnp.concatenate([bh, bm, bh, bm, bl, bh], axis=0),
                (((0,), (0,)), ((), ())),
                preferred_element_type=F32,
            )
            work[base + PANEL :, :] -= update[base + PANEL :, :]
        work[base : base + PANEL, n:] = right * jnp.sqrt(scale)


def solve_kernel(total_rows, meta, gram, split, out, work, result, sem):
    flip = meta[0]
    inverse_factor(gram[...], work)
    spread = (work[:, BS:] * jnp.sqrt(F32(total_rows))).T
    high = spread.astype(BF16)
    low = (spread - high.astype(F32)).astype(BF16)
    half = jnp.concatenate([high, low], axis=1)
    factor = jnp.concatenate([half, half], axis=0)
    steps = 8
    size = OWN // steps
    copies = []
    for step in range(steps):
        rows = split[step * size // 2 : (step + 1) * size // 2].reshape(size * BS, 2 * BS)
        product = jnp.dot(rows, factor, preferred_element_type=F32)
        result[step * size : (step + 1) * size] = (product[:, :BS] + product[:, BS:]).reshape(size, BS, BS)
        copies.append(
            pltpu.make_async_copy(
                result.at[pl.ds(step * size, size)], out.at[pl.ds(step * size ^ flip, size)], sem.at[step]
            )
        )
        copies[-1].start()
    for copy in copies:
        copy.wait()


def swap(pairs, x):
    return lax.ppermute(x, "node", pairs)


def sum_over_node(x, size):
    step = 1
    while step < size:
        x = x + swap([(i, i ^ step) for i in range(size)], x)
        step *= 2
    return x


def local(embed, tiles, tile_rows, tile_cols, tile_count):
    size = lax.axis_size("node")
    device = lax.axis_index("node")
    flip = (device % 2) * HALF
    to_chip = [(i, (i + 1) % size if i % 2 else (i - 1) % size) for i in range(size)]
    to_core = [(i, i ^ 1) for i in range(size)]
    blocks = embed.reshape(OWN, BS, BS)

    cross = lax.dynamic_slice_in_dim(blocks, flip, HALF, 0).astype(BF16)
    cross_in = swap(to_chip, cross)
    inner = lax.dynamic_slice_in_dim(blocks, HALF - flip, HALF, 0).astype(BF16)
    inner_in = swap(to_core, inner)
    order, meta = slot_lists(tile_rows, tile_cols, tile_count, device, flip, size)

    blocks_f32 = vmem(OWN, BS, BS, dtype=F32)
    source = vmem(OWN, BS, BS, dtype=BF16)
    half = vmem(HALF, BS, BS, dtype=BF16)
    work = cost(2 * 96 * BS**3, 8 * MIB)
    total, kept = pl.pallas_call(
        own_first_kernel,
        out_shape=(blocks_f32, vmem(SLOTS + 1, BS, BS, dtype=BF16)),
        in_specs=[S, S, V, V, H, H],
        out_specs=(V, V),
        scratch_shapes=[source, pltpu.SemaphoreType.DMA((3,))],
        compiler_params=params(24),
        cost_estimate=work,
        name="own_first",
    )(order, meta, in_vmem(cross), in_vmem(inner), blocks, tiles)

    first, cross, inner = pl.pallas_call(
        halo_first_kernel,
        out_shape=(blocks_f32, half, half),
        in_specs=[S, S, V, V, V, V],
        out_specs=(V, V, V),
        scratch_shapes=[source],
        compiler_params=params(24),
        cost_estimate=work,
        name="halo_first",
    )(order, meta, in_vmem(cross_in), in_vmem(inner_in), in_vmem(kept), in_vmem(total))

    cross_in = swap(to_chip, cross)
    inner_in = swap(to_core, inner)
    total = pl.pallas_call(
        own_second_kernel,
        out_shape=blocks_f32,
        in_specs=[S, S, V, V, V, V],
        out_specs=V,
        scratch_shapes=[source],
        compiler_params=params(24),
        cost_estimate=work,
        name="own_second",
    )(order, meta, in_vmem(cross), in_vmem(inner), in_vmem(kept), in_vmem(first))

    split, gram = pl.pallas_call(
        halo_second_kernel,
        out_shape=(vmem(OWN // 2, 2 * BS, 2 * BS, dtype=BF16), vmem(BS, BS, dtype=F32)),
        in_specs=[S, S, V, V, V, V, H],
        out_specs=(V, V),
        scratch_shapes=[source, blocks_f32, blocks_f32, pltpu.SemaphoreType.DMA((2,))],
        compiler_params=params(24),
        cost_estimate=work,
        name="halo_second",
    )(order, meta, in_vmem(cross_in), in_vmem(inner_in), in_vmem(kept), in_vmem(total), blocks)

    gram = sum_over_node(gram, size)

    def solve(*refs):
        solve_kernel(embed.shape[0] * size, *refs)

    out = pl.pallas_call(
        solve,
        out_shape=jax.ShapeDtypeStruct((OWN, BS, BS), F32),
        in_specs=[S, V, V],
        out_specs=H,
        scratch_shapes=[vmem(BS, 2 * BS, dtype=F32), blocks_f32, pltpu.SemaphoreType.DMA((8,))],
        compiler_params=params(24),
        name="solve",
    )(meta, in_vmem(gram), in_vmem(split))
    return out.reshape(embed.shape)


def solution(mesh):
    return jax.shard_map(
        local,
        mesh=mesh,
        in_specs=(P("node", None), P("node", None, None), P("node"), P("node"), P("node")),
        out_specs=P("node", None),
        check_vma=False,
    )
```

time: 452 us -> 94.5 us (0.21); the launches traced: 443 us -> 94.8 us
  waiting for transfers between devices: 259 us -> 35.6 us
  matrix products: 83.5 us -> 0 us
  local copies, waits for them, and re-layouts: 49.2 us -> 4.64 us
  other arithmetic: 28.7 us -> 4.14 us
  Pallas kernels: 0 us -> 21.2 us
  starting transfers between devices: 7.85 us -> 28.4 us
  between operations: 14.6 us -> 0.86 us
    psum x1 -> x0, waiting for transfers between devices: 246 us -> none  [local(): gram = lax.psum(inner_gram(mixed, mixed), 'node')]
    dot_general x5 -> x0, matrix products: 77.6 us -> none  [the longest x2 41.1 us: propagate(): jnp.dot(selector, flat, precision=lax.Precision.HIGHEST, preferred_elemen...]
    dot_general x2 -> x0, local copies, waits for them, and re-layouts: 25.2 us -> none  [tile_products(): jnp.einsum('tij,tjf->tif', tiles, picked, preferred_element_type=jnp.floa...]
    ppermute x4 -> x12, waiting for transfers between devices: 13 us -> 35.6 us  [swap(): return lax.ppermute(x, 'node', pairs)]
    pallas_call x0 -> x5, Pallas kernels: none -> 21.2 us  [the longest x1 6.2 us: local(): pl.pallas_call(halo_second_kernel, out_shape=(vmem(OWN // 2, 2 * BS, 2 *...]
    another operation x5 -> x1, other arithmetic: 22.9 us -> 1.94 us  [slot_lists(): meta = jnp.stack([flip, n_own, n_cross, n_halo]).astype(i32)]
    ppermute x4 -> x12, starting transfers between devices: 7.85 us -> 28.4 us  [swap(): return lax.ppermute(x, 'node', pairs)]
    gather x2 -> x0, local copies, waits for them, and re-layouts: 16.2 us -> none  [tile_products(): picked = jnp.take(source, local_cols, axis=0)]
  transfers between devices with their start and end apart: 5 -> 12, of which waited for: 3 -> 9; matrix products, arithmetic and copies ran while one was open for 0% -> 4% of each run, Pallas kernels for 0% -> 6%
where the time goes in v1:
time: 94.5 us; the launch traced here: 94.8 us
  waiting for transfers between devices  35.6 us (38%)
  starting transfers between devices  28.4 us (30%)
  Pallas kernels  21.2 us (22%)
  local copies, waits for them, and re-layouts  4.64 us (5%)
  other arithmetic  4.14 us (4%)
    ppermute x12, waiting for transfers between devices, swap(): return lax.ppermute(x, 'node', pairs)  35.6 us
    ppermute x12, starting transfers between devices, swap(): return lax.ppermute(x, 'node', pairs)  28.4 us
    pallas_call x1, Pallas kernels, local(): pl.pallas_call(halo_second_kernel, out_shape=(vmem(OWN // 2, 2 * BS, 2 *...  6.2 us
    pallas_call x1, Pallas kernels, local(): pl.pallas_call(solve, out_shape=jax.ShapeDtypeStruct((OWN, BS, BS), F32),...  5.76 us
    pallas_call x1, Pallas kernels, local(): pl.pallas_call(halo_first_kernel, out_shape=(blocks_f32, half, half), in_...  3.37 us
    pallas_call x1, Pallas kernels, local(): pl.pallas_call(own_first_kernel, out_shape=(blocks_f32, vmem(SLOTS + 1, B...  3.23 us
    unnamed x8, local copies, waits for them, and re-layouts  2.79 us
    pallas_call x1, Pallas kernels, local(): pl.pallas_call(own_second_kernel, out_shape=blocks_f32, in_specs=[S, S, V...  2.63 us
  transfers between devices with their start and end apart: 12, of which 9 were waited for; matrix products, arithmetic and copies ran while one was open for 4% of the time, Pallas kernels for 6%

profile of v1, /device:TPU:4, one launch (start us, length us, event | category | flops | bytes accessed | tf_op | source)
XLA Modules:
  0.0 94.8 jit_solution(7894673179523763574)
XLA Ops:
  0.0 0.0 copy-start
  0.0 0.0 copy-start.3
  0.0 0.0 copy-start.2
  0.0 1.8 %dynamic-slice_convert_fusion = (bf16[16,128,128]{2,1,0:T(8,128)(2,1)S(1)}, bf16[16,128,128]{2,1,0:T(8,128)(2,1)S(1)}) fusion(f32[32,128,128]{2,1,0:T(8,128)} %bitcast.9, s32[]{:T(128)S(6)} %select_n.67, s32[]{:T(128)S(6)} %select_n.66), kind=kLoop, calls=%fused_computation | loop fusion | bytes 2097160 | tf_op jit(solution)/shard_map/convert_element_type | solution.py:256
  1.9 0.1 collective-permute-start.1
  2.0 3.1 %collective-permute-start = (bf16[16,128,128]{2,1,0:T(8,128)(2,1)S(1)}, bf16[16,128,128]{2,1,0:T(8,128)(2,1)}, u32[]{:S(2)}, u32[]{:S(2)}) collective-permute-start(bf16[16,128,128]{2,1,0:T(8,128)(2,1)S(1)} %get-tuple-element.26.cross), channel_id=1, source_target_pairs={{0,255},{1,2},{2,1},{3,4},{4,3},{5,6},{6,5},{7,8},{8,7},{9,10},{10... | collective-permute-start | bytes 1572872 | tf_op jit(solution)/shard_map/ppermute | solution.py:235
  5.7 0.0 copy-done.3
  5.7 0.0 copy-done.2
  5.8 0.1 convert_reduce_fusion.1
  5.9 0.2 convert_reduce_fusion
  6.1 0.8 slice_reduce_fusion.2
  6.9 0.1 select_reduce_fusion.1
  7.0 0.8 slice_reduce_fusion.1
  7.8 1.9 %pad_add_fusion.meta.refs_0_ = s32[4]{0:T(128)S(1)} fusion(s32[1]{0:T(128)} %bitcast.4, s32[1]{0:T(128)} %bitcast.3, s32[1]{0:T(128)} %bitcast.2, s32[1]{0:T(128)} %bitcast), kind=kLoop, calls=%fused_computation.27 | loop fusion | flops 12 | bytes 32 | tf_op jit(solution)/shard_map/stack | solution.py:76
  9.7 0.1 select_reduce_fusion
  9.8 0.0 copy-done
  9.9 0.0 copy-start.1
  9.9 2.8 %copy-done.1 = bf16[192,128,128]{2,1,0:T(8,128)(2,1)S(1)} copy-done((bf16[192,128,128]{2,1,0:T(8,128)(2,1)S(1)}, bf16[192,128,128]{2,1,0:T(8,128)(2,1)}, u32[]{:S(2)}) %copy-start.1) | copy-done | bytes 6291480
  12.6 3.2 %own_first.1 = (f32[32,128,128]{2,1,0:T(8,128)S(1)}, bf16[193,128,128]{2,1,0:T(8,128)(2,1)S(1)}) custom-call(s32[512]{0:T(512)S(1)} %broadcast_add_fusion.order, s32[4]{0:T(128)S(1)} %pad_add_fusion.meta.refs_0_, bf16[16,128,128]{2,1,0:T(8,128)(2,1)S(1)} %get-tuple-element.26.cross, bf16[16,128,128]{2,1,0:T(8,128)(2,1)S(1)} %get-tuple-element.25.inner, ...), custom_call_target="tpu_custom_call" | custom-call | flops 402653184 | bytes 8388608 | tf_op jit(solution)/shard_map/own_first/pallas_call | solution.py:264
  15.9 0.0 collective-permute-done.1.inner
  15.9 0.0 collective-permute-done.cross
  15.9 3.4 %halo_first.1 = (f32[32,128,128]{2,1,0:T(8,128)S(1)}, bf16[16,128,128]{2,1,0:T(8,128)(2,1)S(1)}, bf16[16,128,128]{2,1,0:T(8,128)(2,1)S(1)}) custom-call(s32[512]{0:T(512)S(1)} %broadcast_add_fusion.order, s32[4]{0:T(128)S(1)} %pad_add_fusion.meta.refs_0_, bf16[16,128,128]{2,1,0:T(8,128)(2,1)} %collective-permute-done.cross, ...), custom_call_target="tpu_custom_call" | custom-call | flops 402653184 | bytes 8388608 | tf_op jit(solution)/shard_map/halo_first/pallas_call | solution.py:275
  19.3 2.3 %collective-permute-start.2 = (bf16[16,128,128]{2,1,0:T(8,128)(2,1)S(1)}, bf16[16,128,128]{2,1,0:T(8,128)(2,1)S(1)}, u32[]{:S(2)}, u32[]{:S(2)}) collective-permute-start(bf16[16,128,128]{2,1,0:T(8,128)(2,1)S(1)} %get-tuple-element.14.cross), channel_id=1, source_target_pairs={{0,255},{1,2},{2,1},{3,4},{4,3},{5,6},{6,5},{7,8},{8,7},{9,10},{10... | collective-permute-start | bytes 1572872 | tf_op jit(solution)/shard_map/ppermute | solution.py:235
  21.6 0.0 collective-permute-start.3
  21.6 2.6 %own_second.1.before = f32[32,128,128]{2,1,0:T(8,128)S(1)} custom-call(s32[512]{0:T(512)S(1)} %broadcast_add_fusion.order, s32[4]{0:T(128)S(1)} %pad_add_fusion.meta.refs_0_, bf16[16,128,128]{2,1,0:T(8,128)(2,1)S(1)} %get-tuple-element.14.cross, bf16[16,128,128]{2,1,0:T(8,128)(2,1)S(1)} %get-tuple-element.15.inner, ...), custom_call_target="tpu_custom_call" | custom-call | flops 402653184 | bytes 8388608 | tf_op jit(solution)/shard_map/own_second/pallas_call | solution.py:288
  24.3 5.8 %collective-permute-done.2.cross = bf16[16,128,128]{2,1,0:T(8,128)(2,1)S(1)} collective-permute-done((bf16[16,128,128]{2,1,0:T(8,128)(2,1)S(1)}, bf16[16,128,128]{2,1,0:T(8,128)(2,1)S(1)}, u32[]{:S(2)}, u32[]{:S(2)}) %collective-permute-start.2) | collective-permute-done | bytes 524320 | tf_op jit(solution)/shard_map/ppermute | solution.py:235
  30.1 0.0 collective-permute-done.3.inner
  30.1 6.2 %halo_second.1 = (bf16[16,256,256]{2,1,0:T(8,128)(2,1)S(1)}, f32[128,128]{1,0:T(8,128)S(1)}) custom-call(s32[512]{0:T(512)S(1)} %broadcast_add_fusion.order, s32[4]{0:T(128)S(1)} %pad_add_fusion.meta.refs_0_, bf16[16,128,128]{2,1,0:T(8,128)(2,1)S(1)} %collective-permute-done.2.cross, bf16[16,128,128]{2,1,0:T(8,128)(2,1)S(1)} %collective-permute-done.3.inner, ...), custom_call_target="tpu_custom_call" | custom-call | flops 402653184 | bytes 8388608 | tf_op jit(solution)/shard_map/halo_second/pallas_call | solution.py:299
  36.3 0.9 collective-permute-start.4
  37.2 0.9 collective-permute-done.4
  38.1 0.1 collective-permute-start.5
  38.2 4.3 %collective-permute-done.5 = f32[128,128]{1,0:T(8,128)S(1)} collective-permute-done((f32[128,128]{1,0:T(8,128)S(1)}, f32[128,128]{1,0:T(8,128)S(1)}, u32[]{:S(2)}, u32[]{:S(2)}) %collective-permute-start.5) | collective-permute-done | bytes 65568 | tf_op jit(solution)/shard_map/ppermute | solution.py:235
  42.6 4.4 %collective-permute-start.6 = (f32[128,128]{1,0:T(8,128)S(1)}, f32[128,128]{1,0:T(8,128)S(1)}, u32[]{:S(2)}, u32[]{:S(2)}) collective-permute-start(f32[128,128]{1,0:T(8,128)S(1)} %add.95), channel_id=1, source_target_pairs={{0,4},{1,5},{2,6},{3,7},{4,0},{5,1},{6,2},{7,3},{8,12},{9,13},{10,... | collective-permute-start | bytes 196616 | tf_op jit(solution)/shard_map/ppermute | solution.py:235
  46.9 2.2 %collective-permute-done.6 = f32[128,128]{1,0:T(8,128)S(1)} collective-permute-done((f32[128,128]{1,0:T(8,128)S(1)}, f32[128,128]{1,0:T(8,128)S(1)}, u32[]{:S(2)}, u32[]{:S(2)}) %collective-permute-start.6) | collective-permute-done | bytes 65568 | tf_op jit(solution)/shard_map/ppermute | solution.py:235
  49.2 2.4 %collective-permute-start.7 = (f32[128,128]{1,0:T(8,128)S(1)}, f32[128,128]{1,0:T(8,128)S(1)}, u32[]{:S(2)}, u32[]{:S(2)}) collective-permute-start(f32[128,128]{1,0:T(8,128)S(1)} %add.96), channel_id=1, source_target_pairs={{0,8},{1,9},{2,10},{3,11},{4,12},{5,13},{6,14},{7,15},{8,0},{9,1},... | collective-permute-start | bytes 196616 | tf_op jit(solution)/shard_map/ppermute | solution.py:235
  51.6 2.2 %collective-permute-done.7 = f32[128,128]{1,0:T(8,128)S(1)} collective-permute-done((f32[128,128]{1,0:T(8,128)S(1)}, f32[128,128]{1,0:T(8,128)S(1)}, u32[]{:S(2)}, u32[]{:S(2)}) %collective-permute-start.7) | collective-permute-done | bytes 65568 | tf_op jit(solution)/shard_map/ppermute | solution.py:235
  53.9 13.5 %collective-permute-start.8 = (f32[128,128]{1,0:T(8,128)S(1)}, f32[128,128]{1,0:T(8,128)S(1)}, u32[]{:S(2)}, u32[]{:S(2)}) collective-permute-start(f32[128,128]{1,0:T(8,128)S(1)} %add.97), channel_id=1, source_target_pairs={{0,16},{1,17},{2,18},{3,19},{4,20},{5,21},{6,22},{7,23},{8,24},{9,... | collective-permute-start | bytes 196616 | tf_op jit(solution)/shard_map/ppermute | solution.py:235
  67.4 2.2 %collective-permute-done.8 = f32[128,128]{1,0:T(8,128)S(1)} collective-permute-done((f32[128,128]{1,0:T(8,128)S(1)}, f32[128,128]{1,0:T(8,128)S(1)}, u32[]{:S(2)}, u32[]{:S(2)}) %collective-permute-start.8) | collective-permute-done | bytes 65568 | tf_op jit(solution)/shard_map/ppermute | solution.py:235
  69.6 0.1 collective-permute-start.9
  69.7 4.7 %collective-permute-done.9 = f32[128,128]{1,0:T(8,128)S(1)} collective-permute-done((f32[128,128]{1,0:T(8,128)S(1)}, f32[128,128]{1,0:T(8,128)S(1)}, u32[]{:S(2)}, u32[]{:S(2)}) %collective-permute-start.9) | collective-permute-done | bytes 65568 | tf_op jit(solution)/shard_map/ppermute | solution.py:235
  74.4 0.1 collective-permute-start.10
  74.5 6.3 %collective-permute-done.10 = f32[128,128]{1,0:T(8,128)S(1)} collective-permute-done((f32[128,128]{1,0:T(8,128)S(1)}, f32[128,128]{1,0:T(8,128)S(1)}, u32[]{:S(2)}, u32[]{:S(2)}) %collective-permute-start.10) | collective-permute-done | bytes 65568 | tf_op jit(solution)/shard_map/ppermute | solution.py:235
  80.8 1.4 %collective-permute-start.11 = (f32[128,128]{1,0:T(8,128)S(1)}, f32[128,128]{1,0:T(8,128)S(1)}, u32[]{:S(2)}, u32[]{:S(2)}) collective-permute-start(f32[128,128]{1,0:T(8,128)S(1)} %add.100), channel_id=1, source_target_pairs={{0,128},{1,129},{2,130},{3,131},{4,132},{5,133},{6,134},{7,135},{8... | collective-permute-start | bytes 196616 | tf_op jit(solution)/shard_map/ppermute | solution.py:235
  82.2 6.8 %collective-permute-done.11 = f32[128,128]{1,0:T(8,128)S(1)} collective-permute-done((f32[128,128]{1,0:T(8,128)S(1)}, f32[128,128]{1,0:T(8,128)S(1)}, u32[]{:S(2)}, u32[]{:S(2)}) %collective-permute-start.11) | collective-permute-done | bytes 65568 | tf_op jit(solution)/shard_map/ppermute | solution.py:235
  89.1 5.8 %solve.1 = f32[32,128,128]{2,1,0:T(8,128)} custom-call(s32[4]{0:T(128)S(1)} %pad_add_fusion.meta.refs_0_, f32[128,128]{1,0:T(8,128)S(1)} %add.101.refs_1_, bf16[16,256,256]{2,1,0:T(8,128)(2,1)S(1)} %get-tuple-element.18.refs_2_), custom_call_target="tpu_custom_call" | custom-call | tf_op jit(solution)/shard_map/solve/pallas_call | solution.py:315
  (13 shorter events, 0.1 us)
Async XLA Ops:
  0.0 9.8 %copy-start = (f32[4096,128]{1,0:T(8,128)S(1)}, f32[4096,128]{1,0:T(8,128)}, u32[]{:S(2)}) copy-start(f32[4096,128]{1,0:T(8,128)} %param.5) | copy-start | bytes 6291460
  0.0 5.7 %copy-start.3 = (s32[192]{0:T(256)S(1)}, s32[192]{0:T(256)}, u32[]{:S(2)}) copy-start(s32[192]{0:T(256)} %param.8) | copy-start | bytes 2308
  0.0 5.7 %copy-start.2 = (s32[192]{0:T(256)S(1)}, s32[192]{0:T(256)}, u32[]{:S(2)}) copy-start(s32[192]{0:T(256)} %param.7) | copy-start | bytes 2308
  1.9 14.0 %collective-permute-start.1 = (bf16[16,128,128]{2,1,0:T(8,128)(2,1)S(1)}, bf16[16,128,128]{2,1,0:T(8,128)(2,1)}, u32[]{:S(2)}, u32[]{:S(2)}) collective-permute-start(bf16[16,128,128]{2,1,0:T(8,128)(2,1)S(1)} %get-tuple-element.25.inner), channel_id=1, source_target_pairs={{0,1},{1,0},{2,3},{3,2},{4,5},{5,4},{6,7},{7,6},{8,9},{9,8},{10,11... | collective-permute-start | bytes 1572872 | tf_op jit(solution)/shard_map/ppermute | solution.py:235
  2.0 13.9 %collective-permute-start = (bf16[16,128,128]{2,1,0:T(8,128)(2,1)S(1)}, bf16[16,128,128]{2,1,0:T(8,128)(2,1)}, u32[]{:S(2)}, u32[]{:S(2)}) collective-permute-start(bf16[16,128,128]{2,1,0:T(8,128)(2,1)S(1)} %get-tuple-element.26.cross), channel_id=1, source_target_pairs={{0,255},{1,2},{2,1},{3,4},{4,3},{5,6},{6,5},{7,8},{8,7},{9,10},{10... | collective-permute-start | bytes 1572872 | tf_op jit(solution)/shard_map/ppermute | solution.py:235
  9.9 2.8 %copy-start.1 = (bf16[192,128,128]{2,1,0:T(8,128)(2,1)S(1)}, bf16[192,128,128]{2,1,0:T(8,128)(2,1)}, u32[]{:S(2)}) copy-start(bf16[192,128,128]{2,1,0:T(8,128)(2,1)} %tiles.1) | copy-start | bytes 18874372
  19.3 10.8 %collective-permute-start.2 = (bf16[16,128,128]{2,1,0:T(8,128)(2,1)S(1)}, bf16[16,128,128]{2,1,0:T(8,128)(2,1)S(1)}, u32[]{:S(2)}, u32[]{:S(2)}) collective-permute-start(bf16[16,128,128]{2,1,0:T(8,128)(2,1)S(1)} %get-tuple-element.14.cross), channel_id=1, source_target_pairs={{0,255},{1,2},{2,1},{3,4},{4,3},{5,6},{6,5},{7,8},{8,7},{9,10},{10... | collective-permute-start | bytes 1572872 | tf_op jit(solution)/shard_map/ppermute | solution.py:235
  21.6 8.5 %collective-permute-start.3 = (bf16[16,128,128]{2,1,0:T(8,128)(2,1)S(1)}, bf16[16,128,128]{2,1,0:T(8,128)(2,1)S(1)}, u32[]{:S(2)}, u32[]{:S(2)}) collective-permute-start(bf16[16,128,128]{2,1,0:T(8,128)(2,1)S(1)} %get-tuple-element.15.inner), channel_id=1, source_target_pairs={{0,1},{1,0},{2,3},{3,2},{4,5},{5,4},{6,7},{7,6},{8,9},{9,8},{10,11... | collective-permute-start | bytes 1572872 | tf_op jit(solution)/shard_map/ppermute | solution.py:235
  36.3 1.8 %collective-permute-start.4 = (f32[128,128]{1,0:T(8,128)S(1)}, f32[128,128]{1,0:T(8,128)S(1)}, u32[]{:S(2)}, u32[]{:S(2)}) collective-permute-start(f32[128,128]{1,0:T(8,128)S(1)} %get-tuple-element.17), channel_id=1, source_target_pairs={{0,1},{1,0},{2,3},{3,2},{4,5},{5,4},{6,7},{7,6},{8,9},{9,8},{10,11... | collective-permute-start | bytes 196616 | tf_op jit(solution)/shard_map/ppermute | solution.py:235
  38.1 4.4 %collective-permute-start.5 = (f32[128,128]{1,0:T(8,128)S(1)}, f32[128,128]{1,0:T(8,128)S(1)}, u32[]{:S(2)}, u32[]{:S(2)}) collective-permute-start(f32[128,128]{1,0:T(8,128)S(1)} %add.94), channel_id=1, source_target_pairs={{0,2},{1,3},{2,0},{3,1},{4,6},{5,7},{6,4},{7,5},{8,10},{9,11},{10,... | collective-permute-start | bytes 196616 | tf_op jit(solution)/shard_map/ppermute | solution.py:235
  42.6 6.6 %collective-permute-start.6 = (f32[128,128]{1,0:T(8,128)S(1)}, f32[128,128]{1,0:T(8,128)S(1)}, u32[]{:S(2)}, u32[]{:S(2)}) collective-permute-start(f32[128,128]{1,0:T(8,128)S(1)} %add.95), channel_id=1, source_target_pairs={{0,4},{1,5},{2,6},{3,7},{4,0},{5,1},{6,2},{7,3},{8,12},{9,13},{10,... | collective-permute-start | bytes 196616 | tf_op jit(solution)/shard_map/ppermute | solution.py:235
  49.2 4.7 %collective-permute-start.7 = (f32[128,128]{1,0:T(8,128)S(1)}, f32[128,128]{1,0:T(8,128)S(1)}, u32[]{:S(2)}, u32[]{:S(2)}) collective-permute-start(f32[128,128]{1,0:T(8,128)S(1)} %add.96), channel_id=1, source_target_pairs={{0,8},{1,9},{2,10},{3,11},{4,12},{5,13},{6,14},{7,15},{8,0},{9,1},... | collective-permute-start | bytes 196616 | tf_op jit(solution)/shard_map/ppermute | solution.py:235
  53.9 15.8 %collective-permute-start.8 = (f32[128,128]{1,0:T(8,128)S(1)}, f32[128,128]{1,0:T(8,128)S(1)}, u32[]{:S(2)}, u32[]{:S(2)}) collective-permute-start(f32[128,128]{1,0:T(8,128)S(1)} %add.97), channel_id=1, source_target_pairs={{0,16},{1,17},{2,18},{3,19},{4,20},{5,21},{6,22},{7,23},{8,24},{9,... | collective-permute-start | bytes 196616 | tf_op jit(solution)/shard_map/ppermute | solution.py:235
  69.6 4.8 %collective-permute-start.9 = (f32[128,128]{1,0:T(8,128)S(1)}, f32[128,128]{1,0:T(8,128)S(1)}, u32[]{:S(2)}, u32[]{:S(2)}) collective-permute-start(f32[128,128]{1,0:T(8,128)S(1)} %add.98), channel_id=1, source_target_pairs={{0,32},{1,33},{2,34},{3,35},{4,36},{5,37},{6,38},{7,39},{8,40},{9,... | collective-permute-start | bytes 196616 | tf_op jit(solution)/shard_map/ppermute | solution.py:235
  74.4 6.4 %collective-permute-start.10 = (f32[128,128]{1,0:T(8,128)S(1)}, f32[128,128]{1,0:T(8,128)S(1)}, u32[]{:S(2)}, u32[]{:S(2)}) collective-permute-start(f32[128,128]{1,0:T(8,128)S(1)} %add.99), channel_id=1, source_target_pairs={{0,64},{1,65},{2,66},{3,67},{4,68},{5,69},{6,70},{7,71},{8,72},{9,... | collective-permute-start | bytes 196616 | tf_op jit(solution)/shard_map/ppermute | solution.py:235
  80.8 8.3 %collective-permute-start.11 = (f32[128,128]{1,0:T(8,128)S(1)}, f32[128,128]{1,0:T(8,128)S(1)}, u32[]{:S(2)}, u32[]{:S(2)}) collective-permute-start(f32[128,128]{1,0:T(8,128)S(1)} %add.100), channel_id=1, source_target_pairs={{0,128},{1,129},{2,130},{3,131},{4,132},{5,133},{6,134},{7,135},{8... | collective-permute-start | bytes 196616 | tf_op jit(solution)/shard_map/ppermute | solution.py:235
